TPU v7x, 32 devices: a whole 2x2x4 slice. The times are simulated.
32 devices in a mesh: batch: 4 (over z), pos: 8 (over y, x, core).
Axes of the slice: x: 2, y: 2, z: 4, core: 2. Of those that a mesh axis runs over, the one named last changes fastest.
Arguments:
- inputs: bfloat16 [4, 4096, 1536], P('batch', 'pos'), may hold values from -6 to 6
- bn_scale: float32 [1536], replicated, may hold values from 0.25 to 1.75
- bn_shift: float32 [1536], replicated, may hold values from -2 to 2
- mid_scale: float32 [384], replicated, may hold values from 0.25 to 1.75
- mid_shift: float32 [384], replicated, may hold values from -2 to 2
- dilated_weight: bfloat16 [1536, 3, 384], P('batch'), may hold values from -0.09375 to 0.09375
- w_point: bfloat16 [384, 1536], P('batch'), may hold values from -0.3125 to 0.3125
- head: bfloat16 [5120, 1536], P('pos'), may hold values from -0.15625 to 0.15625
- targets: bfloat16 [4, 4096, 512], P('batch', 'pos'), may hold values from 0 to 2
- assay_slots: int32 [4, 512], P('batch', 'pos'), may hold values from 0 to 639, as said below
- assay_counts: int32 [4, 8], P('batch', 'pos'), may hold values from 1 to 64, as said below
Outputs:
- d_inputs: bfloat16 [4, 4096, 1536], P('batch', 'pos')
- new_head: bfloat16 [5120, 1536], P('pos')
Inputs may be any that keep to these rules, and one draw needn't show every extreme that they name: `assay_slots`: within each block of 64 slots (one shard of one sequence) the entries are distinct. `assay_counts`: in every sequence some shard has all 64 slots live.
All inputs are finite; a program needn't handle non-finite values.
Results may differ from a plain program's by a relative error of at most 0.012.
Values may be sent and summed in bfloat16 or wider, within the bound.
A program may use at most 64 MiB of HBM per device.

v0:
```python
import jax
import jax.numpy as jnp
from jax import lax
from jax.sharding import PartitionSpec as P

DILATION_STEP = 32


def with_halo(shard, sides, width):
    for axis, dim in sides:
        peers, length = (lax.axis_size(axis), shard.shape[dim])
        up = [(i, (i + 1) % peers) for i in range(peers - 1)]
        down = [(j, i) for i, j in up]
        last = lax.slice_in_dim(shard, length - width, length, axis=dim)
        initial = lax.slice_in_dim(shard, 0, width, axis=dim)
        before = lax.ppermute(last, axis, up)
        after = lax.ppermute(initial, axis, down)
        shard = jnp.concatenate([before, shard, after], axis=dim)
    return shard


def gelu_slope(value):
    return jax.jvp(jax.nn.gelu, (value,), (jnp.ones_like(value),))[1]


def per_device(
    inputs,
    bn_scale,
    bn_shift,
    mid_scale,
    mid_shift,
    dilated_weight,
    w_point,
    head,
    targets,
    assay_slots,
    assay_counts,
):
    contract = (((1,), (1,)), ((), ()))
    kernel, pointwise = (
        lax.all_gather(dilated_weight, "batch", axis=0, tiled=True),
        lax.all_gather(w_point, "batch", axis=0, tiled=True),
    )
    stream = inputs[0]
    rows = stream.shape[0]
    window_length = DILATION_STEP
    first = stream.astype(jnp.float32) * bn_scale + bn_shift
    acted = jax.nn.gelu(first).astype(jnp.bfloat16)
    padded_input = with_halo(acted, (("pos", 0),), window_length)
    hidden_state = jnp.dot(
        padded_input[0:rows], kernel[:, 0, :], preferred_element_type=jnp.float32
    )
    hidden_state = hidden_state + jnp.dot(
        padded_input[window_length : window_length + rows],
        kernel[:, 1, :],
        preferred_element_type=jnp.float32,
    )
    hidden_state = hidden_state + jnp.dot(
        padded_input[2 * window_length : 2 * window_length + rows],
        kernel[:, 2, :],
        preferred_element_type=jnp.float32,
    )
    second = hidden_state * mid_scale + mid_shift
    mid = jax.nn.gelu(second).astype(jnp.bfloat16)
    embed = (
        stream.astype(jnp.float32) + jnp.dot(mid, pointwise, preferred_element_type=jnp.float32)
    ).astype(jnp.bfloat16)
    slots = assay_slots[0]
    slot_count = slots.shape[0]
    chosen = head[slots]
    live_mark = (jnp.arange(slot_count) < assay_counts[0, 0]).astype(jnp.bfloat16)
    selected, live_all = (
        lax.all_gather(chosen, "pos", axis=0, tiled=True),
        lax.all_gather(live_mark, "pos", axis=0, tiled=True),
    )
    pre = lax.dot_general(embed, selected, contract, preferred_element_type=jnp.float32)
    goal = targets[0].astype(jnp.float32)
    delta = (
        live_all.astype(jnp.float32) * (jax.nn.softplus(pre) - goal) * jax.nn.sigmoid(pre)
    ).astype(jnp.bfloat16)
    back = jnp.dot(delta, selected, preferred_element_type=jnp.float32).astype(jnp.bfloat16)
    dmid = lax.dot_general(back, pointwise, contract, preferred_element_type=jnp.float32)
    dhid = (dmid * gelu_slope(second) * mid_scale).astype(jnp.bfloat16)
    padded_grad = with_halo(dhid, (("pos", 0),), window_length)
    dact = lax.dot_general(
        padded_grad[2 * window_length : 2 * window_length + rows],
        kernel[:, 0, :],
        contract,
        preferred_element_type=jnp.float32,
    )
    dact = dact + lax.dot_general(
        padded_grad[window_length : window_length + rows],
        kernel[:, 1, :],
        contract,
        preferred_element_type=jnp.float32,
    )
    dact = dact + lax.dot_general(
        padded_grad[0:rows], kernel[:, 2, :], contract, preferred_element_type=jnp.float32
    )
    d_inputs = (back.astype(jnp.float32) + dact * gelu_slope(first) * bn_scale).astype(jnp.bfloat16)
    owned = lax.psum_scatter(
        lax.dot_general(
            delta, embed, (((0,), (0,)), ((), ())), preferred_element_type=jnp.float32
        ).astype(jnp.bfloat16),
        "pos",
        scatter_dimension=0,
        tiled=True,
    ).astype(jnp.float32)
    spread = jnp.zeros((head.shape[0], owned.shape[1]), jnp.float32).at[slots].add(owned)
    d_head = lax.psum(spread.astype(jnp.bfloat16), "batch").astype(jnp.float32)
    new_head = (head.astype(jnp.float32) - 0.004 * d_head).astype(jnp.bfloat16)
    return (d_inputs[None], new_head)


def solution(mesh):
    in_specs = (
        P("batch", "pos", None),
        P(),
        P(),
        P(),
        P(),
        P("batch", None, None),
        P("batch", None),
        P("pos", None),
        P("batch", "pos", None),
        P("batch", "pos"),
        P("batch", "pos"),
    )
    out_specs = (P("batch", "pos", None), P("pos", None))
    return jax.shard_map(
        per_device, mesh=mesh, in_specs=in_specs, out_specs=out_specs, check_vma=False
    )
```

profile of v0, /device:TPU:0, one launch (start us, length us, event | category | flops | bytes accessed | tf_op | source)
XLA Modules:
  0.0 286.1 jit_solution(2264082619135657359)
XLA Ops:
  7.3 0.7 all-gather.5.cloned.1.call-update
  8.0 0.7 all-gather.7.cloned.1.call-update
  8.7 0.7 fusion.71
  9.4 3.4 %gather_fusion = bf16[64,1536]{1,0:T(8,128)(2,1)} fusion(bf16[640,1536]{1,0:T(8,128)(2,1)} %param.18, s32[1024]{0:T(1024)S(1)} %pad_clamp_fusion), kind=kCustom, calls=%fused_computation | custom fusion | bytes 393472 | tf_op jit(solution)/shard_map/gather | solution.py:70
  12.9 1.3 fusion.12
  14.2 2.4 collective-permute-start
  16.6 1.3 collective-permute-start.1
  18.5 0.6 dynamic-slice
  19.9 17.5 %all-reduce = bf16[512]{0:T(512)(128)(2,1)S(1)} all-reduce(bf16[512]{0:T(512)(128)(2,1)S(1)} %dynamic-update-slice), channel_id=1, replica_groups=mesh['batch'=4,'pos'=8] {'pos'}, use_global_device_ids=true, to_apply=%add | all-reduce | flops 512 | bytes 2048
  37.4 44.9 %all-gather.5.cloned.1.call-done = bf16[1536,3,384]{2,0,1:T(8,128)(2,1)} async-done(((bf16[384,3,384]{2,0,1:T(8,128)(2,1)}), bf16[1536,3,384]{2,0,1:T(8,128)(2,1)}) %all-gather.5.cloned.1.call-update) | async-done | bytes 3538960 | tf_op jit(solution)/shard_map/all_gather | solution.py:41
  82.3 2.8 fusion.38
  85.2 1.9 fusion.34
  87.1 1.9 fusion.44
  89.0 23.9 %all-gather.7.cloned.1.call-done = bf16[384,1536]{1,0:T(8,128)(2,1)} async-done(((bf16[96,1536]{1,0:T(8,128)(2,1)}), bf16[384,1536]{1,0:T(8,128)(2,1)}) %all-gather.7.cloned.1.call-update) | async-done | bytes 1179664 | tf_op jit(solution)/shard_map/all_gather | solution.py:42
  113.0 2.5 fusion.29
  115.5 24.8 %all-gather.9.cloned.1.call-done = bf16[512,1536]{1,0:T(8,128)(2,1)} async-done(((bf16[64,1536]{1,0:T(8,128)(2,1)}), bf16[512,1536]{1,0:T(8,128)(2,1)}) %all-gather.9.cloned.1.call-update) | async-done | bytes 1572880 | tf_op jit(solution)/shard_map/all_gather | solution.py:73
  140.3 2.5 fusion.90
  142.8 1.0 copy-done.13
  143.7 4.3 %convolution_convert_fusion = bf16[512,1536]{1,0:T(8,128)(2,1)} fusion(bf16[512,1536]{1,0:T(8,128)(2,1)} %copy-done.12, f32[512,512]{1,0:T(8,128)S(1)} %fusion.90, bf16[1,512,512]{2,1,0:T(8,128)(2,1)S(1)} %copy-done.8, f32[512]{0:T(512)S(1)} %convert_element_type.70), kind=kOutput, calls=%fused_computation.39 | convolution fusion | flops 809762816 | bytes 4720640 | tf_op jit(solution)/shard_map/dot_general | solution.py:102
  148.2 4.1 %convolution_convert_fusion.1 = bf16[512,1536]{1,0:T(8,128)(2,1)} fusion(bf16[512,1536]{1,0:T(8,128)(2,1)S(1)} %copy-done.6, f32[512,512]{1,0:T(8,128)} %copy-done.13, bf16[1,512,512]{2,1,0:T(8,128)(2,1)} %param.19, f32[512]{0:T(512)S(1)} %convert_element_type.70), kind=kOutput, calls=%fused_computation.40 | convolution fusion | flops 809762816 | bytes 4720640 | tf_op jit(solution)/shard_map/dot_general | solution.py:81
  152.2 34.5 %reduce-scatter.2.cloned.1.call-done = bf16[64,1536]{1,0:T(8,128)(2,1)} async-done(((bf16[512,1536]{1,0:T(8,128)(2,1)}), bf16[64,1536]{1,0:T(8,128)(2,1)}) %reduce-scatter.2.cloned.1.call-update) | async-done | bytes 196624 | tf_op jit(solution)/shard_map/reduce_scatter | solution.py:101
  186.7 3.7 %scatter_custom_fusion = f32[640,1536]{1,0:T(8,128)} fusion(s32[64]{0:T(128)S(1)} %fusion.71, f32[]{:T(128)} %constant.15.clone.1, bf16[64,1536]{1,0:T(8,128)(2,1)} %reduce-scatter.2.cloned.1.call-done), kind=kCustom, calls=%fused_computation.43 | custom fusion | flops 196608 | bytes 4128772 | tf_op jit(solution)/shard_map/scatter-add | solution.py:109
  190.4 3.7 %convert_element_type.89 = bf16[640,1536]{1,0:T(8,128)(2,1)} convert(f32[640,1536]{1,0:T(8,128)} %scatter_custom_fusion) | non-fusion elementwise | flops 983040 | bytes 5898240 | tf_op jit(solution)/shard_map/convert_element_type | solution.py:110
  194.1 3.0 %fusion.45 = bf16[512,384]{1,0:T(8,128)(2,1)S(1)} fusion(bf16[512,1536]{1,0:T(8,128)(2,1)} %convolution_convert_fusion.1, bf16[384,1536]{1,0:T(8,128)(2,1)S(1)} %copy-done.7, f32[512,384]{1,0:T(8,128)} %fusion.44, f32[384]{0:T(512)S(1)} %copy-done.10), kind=kOutput, calls=%fused_computation.59 | convolution fusion | flops 607715328 | bytes 3933696 | tf_op jit(solution)/shard_map/dot_general | solution.py:82
  197.2 1.3 collective-permute-start.2
  198.5 3.0 %collective-permute-start.3 = (bf16[32,384]{1,0:T(8,128)(2,1)S(1)}, bf16[32,384]{1,0:T(8,128)(2,1)S(1)}, u32[]{:S(2)}, u32[]{:S(2)}) collective-permute-start(bf16[32,384]{1,0:T(8,128)(2,1)S(1)} %get-tuple-element.5), channel_id=1, source_target_pairs={{0,1},{1,2},{2,3},{3,4},{4,5},{5,6},{6,7},{8,9},{9,10},{10,11},{11... | collective-permute-start | bytes 73736 | tf_op jit(solution)/shard_map/ppermute | solution.py:16
  201.5 1.0 fusion.50
  202.6 1.0 fusion.51
  203.6 0.3 copy-done.14
  204.0 4.0 %fusion.30 = bf16[1,512,1536]{2,1,0:T(8,128)(2,1)} fusion(bf16[1,512,1536]{2,1,0:T(8,128)(2,1)S(1)} %copy-done.1, f32[512,1536]{1,0:T(8,128)S(1)} %fusion.51, f32[512,1536]{1,0:T(8,128)S(1)} %fusion.50, bf16[512,1536]{1,0:T(8,128)(2,1)S(1)} %copy-done.14, f32[1536]{0:T(1024)S(1)} %copy-done.4, f32[1536]{0:T(1024)S(1)} %copy-done.5, ...), kind=kOutput, calls=%fused_computation.42 | convolution fusion | flops 625213440 | bytes 12623872 | tf_op jit(solution)/shard_map/dot_general | solution.py:85
  207.9 68.3 %all-reduce.3.cloned.1.call-done = bf16[640,1536]{1,0:T(8,128)(2,1)} async-done(((bf16[640,1536]{1,0:T(8,128)(2,1)}), bf16[640,1536]{1,0:T(8,128)(2,1)}) %all-reduce.3.cloned.1.call-update) | async-done | bytes 1966096 | tf_op jit(solution)/shard_map/psum | solution.py:110
  276.2 3.4 %subtract_convert_fusion = bf16[640,1536]{1,0:T(8,128)(2,1)} fusion(bf16[640,1536]{1,0:T(8,128)(2,1)} %all-reduce.3.cloned.1.call-done, bf16[640,1536]{1,0:T(8,128)(2,1)S(1)} %copy-done), kind=kLoop, calls=%fused_computation.9 | loop fusion | flops 4915200 | bytes 5898240 | tf_op jit(solution)/shard_map/convert_element_type | solution.py:111
  (47 shorter events, 0.6 us)
Async XLA Ops:
  7.2 11.4 %copy-start.11 = (u32[32]{0:T(128)S(1)}, u32[32]{0:T(128)}, u32[]{:S(2)}) copy-start(u32[32]{0:T(128)} %constant.34) | copy-start | bytes 388
  7.2 5.7 %copy-start.1 = (bf16[1,512,1536]{2,1,0:T(8,128)(2,1)S(1)}, bf16[1,512,1536]{2,1,0:T(8,128)(2,1)}, u32[]{:S(2)}) copy-start(bf16[1,512,1536]{2,1,0:T(8,128)(2,1)} %param.11) | copy-start | bytes 4718596
  7.2 5.7 %copy-start.4 = (f32[1536]{0:T(1024)S(1)}, f32[1536]{0:T(1024)}, u32[]{:S(2)}) copy-start(f32[1536]{0:T(1024)} %param.13) | copy-start | bytes 18436
  7.2 5.7 %copy-start.5 = (f32[1536]{0:T(1024)S(1)}, f32[1536]{0:T(1024)}, u32[]{:S(2)}) copy-start(f32[1536]{0:T(1024)} %param.12) | copy-start | bytes 18436
  7.2 75.1 %all-gather.5.cloned.1.call-start = ((), (), s32[]{:S(2)}) async-start(), calls=%async_computation.1 | async-start | bytes 4423680 | tf_op jit(solution)/shard_map/all_gather | solution.py:41
  7.9 105.0 %all-gather.7.cloned.1.call-start = ((), (), s32[]{:S(2)}) async-start(), calls=%async_computation.2 | async-start | bytes 1474560 | tf_op jit(solution)/shard_map/all_gather | solution.py:42
  8.7 131.6 %all-gather.9.cloned.1.call-start = ((), (), s32[]{:S(2)}) async-start(), calls=%async_computation.5 | async-start | bytes 1769472 | tf_op jit(solution)/shard_map/all_gather | solution.py:73
  12.8 173.9 %reduce-scatter.2.cloned.1.call-start = ((), (), s32[]{:S(2)}) async-start(), calls=%async_computation.3 | async-start | bytes 1769472 | tf_op jit(solution)/shard_map/reduce_scatter | solution.py:101
  14.2 72.9 %collective-permute-start = (bf16[32,1536]{1,0:T(8,128)(2,1)S(1)}, bf16[32,1536]{1,0:T(8,128)(2,1)S(1)}, u32[]{:S(2)}, u32[]{:S(2)}) collective-permute-start(bf16[32,1536]{1,0:T(8,128)(2,1)S(1)} %get-tuple-element.2), channel_id=1, source_target_pairs={{0,1},{1,2},{2,3},{3,4},{4,5},{5,6},{6,7},{8,9},{9,10},{10,11},{11... | collective-permute-start | bytes 294920 | tf_op jit(solution)/shard_map/ppermute | solution.py:16
  16.6 68.6 %collective-permute-start.1 = (bf16[32,1536]{1,0:T(8,128)(2,1)S(1)}, bf16[32,1536]{1,0:T(8,128)(2,1)}, u32[]{:S(2)}, u32[]{:S(2)}) collective-permute-start(bf16[32,1536]{1,0:T(8,128)(2,1)S(1)} %get-tuple-element.3), channel_id=1, source_target_pairs={{1,0},{2,1},{3,2},{4,3},{5,4},{6,5},{7,6},{9,8},{10,9},{11,10},{12... | collective-permute-start | bytes 294920 | tf_op jit(solution)/shard_map/ppermute | solution.py:17
  82.3 2.9 %copy-start.2 = (bf16[1536,3,384]{2,0,1:T(8,128)(2,1)S(1)}, bf16[1536,3,384]{2,0,1:T(8,128)(2,1)}, u32[]{:S(2)}) copy-start(bf16[1536,3,384]{2,0,1:T(8,128)(2,1)} %all-gather.5.cloned.1.call-done) | copy-start | bytes 10616836
  85.1 1.9 copy-start.9
  85.2 1.9 copy-start.10
  115.5 24.8 %copy-start.12 = (bf16[512,1536]{1,0:T(8,128)(2,1)}, bf16[512,1536]{1,0:T(8,128)(2,1)S(1)}, u32[]{:S(2)}) copy-start(bf16[512,1536]{1,0:T(8,128)(2,1)S(1)} %fusion.29) | copy-start | bytes 4718596
  140.3 3.5 %copy-start.8 = (bf16[1,512,512]{2,1,0:T(8,128)(2,1)S(1)}, bf16[1,512,512]{2,1,0:T(8,128)(2,1)}, u32[]{:S(2)}) copy-start(bf16[1,512,512]{2,1,0:T(8,128)(2,1)} %param.19) | copy-start | bytes 1572868
  142.8 1.0 copy-start.13
  143.7 4.4 %copy-start.6 = (bf16[512,1536]{1,0:T(8,128)(2,1)S(1)}, bf16[512,1536]{1,0:T(8,128)(2,1)}, u32[]{:S(2)}) copy-start(bf16[512,1536]{1,0:T(8,128)(2,1)} %all-gather.9.cloned.1.call-done) | copy-start | bytes 4718596
  148.1 128.1 %all-reduce.3.cloned.1.call-start = ((), (), s32[]{:S(2)}) async-start(), calls=%async_computation.4 | async-start | bytes 3932160 | tf_op jit(solution)/shard_map/psum | solution.py:110
  190.4 3.7 %copy-start.7 = (bf16[384,1536]{1,0:T(8,128)(2,1)S(1)}, bf16[384,1536]{1,0:T(8,128)(2,1)}, u32[]{:S(2)}) copy-start(bf16[384,1536]{1,0:T(8,128)(2,1)} %all-gather.7.cloned.1.call-done) | copy-start | bytes 3538948
  194.1 7.4 %copy-start.3 = (bf16[1536,3,384]{2,0,1:T(8,128)(2,1)S(1)}, bf16[1536,3,384]{2,0,1:T(8,128)(2,1)}, u32[]{:S(2)}) copy-start(bf16[1536,3,384]{2,0,1:T(8,128)(2,1)} %all-gather.5.cloned.1.call-done) | copy-start | bytes 10616836
  197.2 6.4 %collective-permute-start.2 = (bf16[32,384]{1,0:T(8,128)(2,1)S(1)}, bf16[32,384]{1,0:T(8,128)(2,1)S(1)}, u32[]{:S(2)}, u32[]{:S(2)}) collective-permute-start(bf16[32,384]{1,0:T(8,128)(2,1)S(1)} %get-tuple-element.4), channel_id=1, source_target_pairs={{1,0},{2,1},{3,2},{4,3},{5,4},{6,5},{7,6},{9,8},{10,9},{11,10},{12... | collective-permute-start | bytes 73736 | tf_op jit(solution)/shard_map/ppermute | solution.py:17
  198.5 4.1 %collective-permute-start.3 = (bf16[32,384]{1,0:T(8,128)(2,1)S(1)}, bf16[32,384]{1,0:T(8,128)(2,1)S(1)}, u32[]{:S(2)}, u32[]{:S(2)}) collective-permute-start(bf16[32,384]{1,0:T(8,128)(2,1)S(1)} %get-tuple-element.5), channel_id=1, source_target_pairs={{0,1},{1,2},{2,3},{3,4},{4,5},{5,6},{6,7},{8,9},{9,10},{10,11},{11... | collective-permute-start | bytes 73736 | tf_op jit(solution)/shard_map/ppermute | solution.py:16
  202.5 1.4 copy-start.14
  203.6 72.6 %copy-start = (bf16[640,1536]{1,0:T(8,128)(2,1)S(1)}, bf16[640,1536]{1,0:T(8,128)(2,1)}, u32[]{:S(2)}) copy-start(bf16[640,1536]{1,0:T(8,128)(2,1)} %param.18) | copy-start | bytes 5898244
Sparse Core Ops, SparseCore 0:
  9.6 72.6 all-gather.4
  83.9 29.0 all-gather.6
  115.4 24.7 all-gather.8
  148.2 38.4 reduce-scatter.1
  194.2 81.9 all-reduce.2
where the time goes:
time: 287 us; the launch traced here: 286 us
  waiting for transfers between devices  198 us (69%)
  matrix products  29 us (10%)
  blocking collectives  17.5 us (6%)
  between operations  15.3 us (5%)
  other arithmetic  12.7 us (4%)
  starting transfers between devices  8.18 us (3%)
  local copies, waits for them, and re-layouts  5.62 us (2%)
    psum x1, waiting for transfers between devices, per_device(): d_head = lax.psum(spread.astype(jnp.bfloat16), 'batch').astype(jnp.float32)  68.3 us
    all_gather x1, waiting for transfers between devices, per_device(): lax.all_gather(dilated_weight, 'batch', axis=0, tiled=True)  44.9 us
    reduce_scatter x1, waiting for transfers between devices, per_device(): lax.psum_scatter(lax.dot_general(delta, embed, (((0,), (0,)), ((), ())),...  34.5 us
    all_gather x1, waiting for transfers between devices, per_device(): lax.all_gather(chosen, 'pos', axis=0, tiled=True)  24.8 us
    all_gather x1, waiting for transfers between devices, per_device(): lax.all_gather(w_point, 'batch', axis=0, tiled=True)  23.9 us
    unnamed x1, blocking collectives  17.5 us
  transfers between devices with their start and end apart: 9, of which 5 were waited for; matrix products, arithmetic and copies ran while one was open for 10% of the time, Pallas kernels for 0%

commit v1 on v0

--- a/solution.py
+++ b/solution.py
@@ -107,7 +107,9 @@
         tiled=True,
     ).astype(jnp.float32)
     spread = jnp.zeros((head.shape[0], owned.shape[1]), jnp.float32).at[slots].add(owned)
-    d_head = lax.psum(spread.astype(jnp.bfloat16), "batch").astype(jnp.float32)
+    d_head = jnp.sum(lax.all_gather(spread.astype(jnp.bfloat16), "batch"), axis=0).astype(
+        jnp.float32
+    )
     new_head = (head.astype(jnp.float32) - 0.004 * d_head).astype(jnp.bfloat16)
     return (d_inputs[None], new_head)
 

time: 287 us -> 350 us (1.22)
  waiting for transfers between devices: 198 us -> 259 us
  other arithmetic: 12.7 us -> 18.5 us
    all_gather x0 -> x1, waiting for transfers between devices: none -> 126 us  [per_device(): lax.all_gather(spread.astype(jnp.bfloat16), 'batch')]
    psum x1 -> x0, waiting for transfers between devices: 68.3 us -> none  [per_device(): d_head = lax.psum(spread.astype(jnp.bfloat16), 'batch').astype(jnp.float32)]
    reduce_sum x0 -> x1, other arithmetic: none -> 5.73 us  [per_device(): jnp.sum(lax.all_gather(spread.astype(jnp.bfloat16), 'batch'), axis=0)]
    reduce_scatter x1, waiting for transfers between devices: 34.5 us -> 38.6 us  [per_device(): lax.psum_scatter(lax.dot_general(delta, embed, (((0,), (0,)), ((), ())),...]
  transfers between devices with their start and end apart: 9 -> 9, of which waited for: 5 -> 5; matrix products, arithmetic and copies ran while one was open for 10% -> 8% of each run, Pallas kernels for 0% -> 0%
where the time goes in v1:
time: 350 us; the launch traced here: 349 us
  waiting for transfers between devices  259 us (74%)
  matrix products  26.4 us (8%)
  other arithmetic  18.5 us (5%)
  blocking collectives  17.4 us (5%)
  between operations  15.4 us (4%)
  starting transfers between devices  8.17 us (2%)
  local copies, waits for them, and re-layouts  4.32 us (1%)
    all_gather x1, waiting for transfers between devices, per_device(): lax.all_gather(spread.astype(jnp.bfloat16), 'batch')  126 us
    all_gather x1, waiting for transfers between devices, per_device(): lax.all_gather(dilated_weight, 'batch', axis=0, tiled=True)  44.8 us
    reduce_scatter x1, waiting for transfers between devices, per_device(): lax.psum_scatter(lax.dot_general(delta, embed, (((0,), (0,)), ((), ())),...  38.6 us
    all_gather x1, waiting for transfers between devices, per_device(): lax.all_gather(w_point, 'batch', axis=0, tiled=True)  24 us
    all_gather x1, waiting for transfers between devices, per_device(): lax.all_gather(chosen, 'pos', axis=0, tiled=True)  23.6 us
    unnamed x1, blocking collectives  17.4 us
  transfers between devices with their start and end apart: 9, of which 5 were waited for; matrix products, arithmetic and copies ran while one was open for 8% of the time, Pallas kernels for 0%

profile of v1, /device:TPU:0, one launch (start us, length us, event | category | flops | bytes accessed | tf_op | source)
XLA Modules:
  0.0 349.1 jit_solution(9968634959571004362)
XLA Ops:
  7.3 0.7 all-gather.7.cloned.1.call-update
  8.0 0.7 all-gather.9.cloned.1.call-update
  8.7 0.7 fusion.71
  9.4 3.4 gather_fusion
  12.9 1.3 fusion.12
  14.2 2.4 collective-permute-start
  16.6 1.3 collective-permute-start.1
  18.5 0.6 dynamic-slice
  19.8 0.2 dynamic-update-slice
  20.0 17.4 %all-reduce = bf16[512]{0:T(512)(128)(2,1)S(1)} all-reduce(bf16[512]{0:T(512)(128)(2,1)S(1)} %dynamic-update-slice), channel_id=1, replica_groups=mesh['batch'=4,'pos'=8] {'pos'}, use_global_device_ids=true, to_apply=%add | all-reduce | flops 512 | bytes 2048
  37.5 44.8 %all-gather.7.cloned.1.call-done = bf16[1536,3,384]{2,0,1:T(8,128)(2,1)} async-done(((bf16[384,3,384]{2,0,1:T(8,128)(2,1)}), bf16[1536,3,384]{2,0,1:T(8,128)(2,1)}) %all-gather.7.cloned.1.call-update) | async-done | bytes 3538960 | tf_op jit(solution)/shard_map/all_gather | solution.py:41
  82.3 2.8 fusion.38
  85.2 1.9 fusion.34
  87.1 1.9 fusion.44
  89.0 24.0 %all-gather.9.cloned.1.call-done = bf16[384,1536]{1,0:T(8,128)(2,1)} async-done(((bf16[96,1536]{1,0:T(8,128)(2,1)}), bf16[384,1536]{1,0:T(8,128)(2,1)}) %all-gather.9.cloned.1.call-update) | async-done | bytes 1179664 | tf_op jit(solution)/shard_map/all_gather | solution.py:42
  113.0 3.7 %fusion.29 = bf16[512,1536]{1,0:T(8,128)(2,1)} fusion(bf16[384,1536]{1,0:T(8,128)(2,1)} %all-gather.9.cloned.1.call-done, bf16[1,512,1536]{2,1,0:T(8,128)(2,1)S(1)} %copy-done, f32[512,384]{1,0:T(8,128)} %fusion.44), kind=kOutput, calls=%fused_computation.41 | convolution fusion | flops 608108544 | bytes 5111808 | tf_op jit(solution)/shard_map/dot_general | solution.py:66
  116.6 23.6 %all-gather.11.cloned.1.call-done = bf16[512,1536]{1,0:T(8,128)(2,1)} async-done(((bf16[64,1536]{1,0:T(8,128)(2,1)}), bf16[512,1536]{1,0:T(8,128)(2,1)}) %all-gather.11.cloned.1.call-update) | async-done | bytes 1572880 | tf_op jit(solution)/shard_map/all_gather | solution.py:73
  140.3 3.0 fusion.90
  143.3 2.8 convolution_convert_fusion
  146.2 38.6 %reduce-scatter.2.cloned.1.call-done = bf16[64,1536]{1,0:T(8,128)(2,1)} async-done(((bf16[512,1536]{1,0:T(8,128)(2,1)}), bf16[64,1536]{1,0:T(8,128)(2,1)}) %reduce-scatter.2.cloned.1.call-update) | async-done | bytes 196624 | tf_op jit(solution)/shard_map/reduce_scatter | solution.py:101
  184.8 3.7 %scatter_custom_fusion = f32[640,1536]{1,0:T(8,128)} fusion(s32[64]{0:T(128)S(1)} %fusion.71, f32[]{:T(128)} %constant.16.clone.1, bf16[64,1536]{1,0:T(8,128)(2,1)} %reduce-scatter.2.cloned.1.call-done), kind=kCustom, calls=%fused_computation.43 | custom fusion | flops 196608 | bytes 4128772 | tf_op jit(solution)/shard_map/scatter-add | solution.py:109
  188.5 3.7 %convert_element_type.91 = bf16[640,1536]{1,0:T(8,128)(2,1)} convert(f32[640,1536]{1,0:T(8,128)} %scatter_custom_fusion) | non-fusion elementwise | flops 983040 | bytes 5898240 | tf_op jit(solution)/shard_map/convert_element_type | solution.py:110
  192.3 3.0 convolution_convert_fusion.1
  195.3 1.3 fusion.45
  196.6 1.3 collective-permute-start.2
  197.9 3.0 collective-permute-start.3
  201.0 1.0 fusion.50
  202.0 1.0 fusion.51
  203.0 4.0 %fusion.30 = bf16[1,512,1536]{2,1,0:T(8,128)(2,1)} fusion(bf16[1,512,1536]{2,1,0:T(8,128)(2,1)S(1)} %copy-done, f32[512,1536]{1,0:T(8,128)S(1)} %fusion.51, f32[512,1536]{1,0:T(8,128)S(1)} %fusion.50, bf16[512,1536]{1,0:T(8,128)(2,1)S(1)} %convolution_convert_fusion.1, f32[1536]{0:T(1024)S(1)} %copy-done.3, f32[1536]{0:T(1024)S(1)} %copy-done.4, ...), kind=kOutput, calls=%fused_computation.42 | convolution fusion | flops 625213440 | bytes 12623872 | tf_op jit(solution)/shard_map/dot_general | solution.py:85
  207.0 126.4 %all-gather.13.cloned.1.call-done = bf16[2560,1536]{1,0:T(8,128)(2,1)} async-done(((bf16[640,1536]{1,0:T(8,128)(2,1)}), bf16[2560,1536]{1,0:T(8,128)(2,1)}) %all-gather.13.cloned.1.call-update) | async-done | bytes 7864336 | tf_op jit(solution)/shard_map/all_gather | solution.py:110
  333.4 5.7 %reduce_sum.12 = bf16[640,1536]{1,0:T(8,128)(2,1)S(1)} reduce(bf16[4,640,1536]{2,1,0:T(8,128)(2,1)} %bitcast.94, bf16[]{:T(256)} %constant.5.clone.1), dimensions={0}, to_apply=%region_2.3 | reduce | flops 2949120 | bytes 9830402 | tf_op jit(solution)/shard_map/reduce_sum | solution.py:110
  339.2 3.4 subtract_convert_fusion
  (46 shorter events, 0.4 us)
Async XLA Ops:
  7.2 11.4 %copy-start.10 = (u32[32]{0:T(128)S(1)}, u32[32]{0:T(128)}, u32[]{:S(2)}) copy-start(u32[32]{0:T(128)} %constant.37) | copy-start | bytes 388
  7.2 5.7 %copy-start = (bf16[1,512,1536]{2,1,0:T(8,128)(2,1)S(1)}, bf16[1,512,1536]{2,1,0:T(8,128)(2,1)}, u32[]{:S(2)}) copy-start(bf16[1,512,1536]{2,1,0:T(8,128)(2,1)} %param.11) | copy-start | bytes 4718596
  7.2 5.7 %copy-start.3 = (f32[1536]{0:T(1024)S(1)}, f32[1536]{0:T(1024)}, u32[]{:S(2)}) copy-start(f32[1536]{0:T(1024)} %param.13) | copy-start | bytes 18436
  7.2 5.7 %copy-start.4 = (f32[1536]{0:T(1024)S(1)}, f32[1536]{0:T(1024)}, u32[]{:S(2)}) copy-start(f32[1536]{0:T(1024)} %param.12) | copy-start | bytes 18436
  7.2 75.1 %all-gather.7.cloned.1.call-start = ((), (), s32[]{:S(2)}) async-start(), calls=%async_computation.1 | async-start | bytes 4423680 | tf_op jit(solution)/shard_map/all_gather | solution.py:41
  7.9 105.0 %all-gather.9.cloned.1.call-start = ((), (), s32[]{:S(2)}) async-start(), calls=%async_computation.2 | async-start | bytes 1474560 | tf_op jit(solution)/shard_map/all_gather | solution.py:42
  8.7 131.6 %all-gather.11.cloned.1.call-start = ((), (), s32[]{:S(2)}) async-start(), calls=%async_computation.4 | async-start | bytes 1769472 | tf_op jit(solution)/shard_map/all_gather | solution.py:73
  12.8 172.0 %reduce-scatter.2.cloned.1.call-start = ((), (), s32[]{:S(2)}) async-start(), calls=%async_computation.3 | async-start | bytes 1769472 | tf_op jit(solution)/shard_map/reduce_scatter | solution.py:101
  14.2 72.9 %collective-permute-start = (bf16[32,1536]{1,0:T(8,128)(2,1)S(1)}, bf16[32,1536]{1,0:T(8,128)(2,1)S(1)}, u32[]{:S(2)}, u32[]{:S(2)}) collective-permute-start(bf16[32,1536]{1,0:T(8,128)(2,1)S(1)} %get-tuple-element.2), channel_id=1, source_target_pairs={{0,1},{1,2},{2,3},{3,4},{4,5},{5,6},{6,7},{8,9},{9,10},{10,11},{11... | collective-permute-start | bytes 294920 | tf_op jit(solution)/shard_map/ppermute | solution.py:16
  16.6 68.6 %collective-permute-start.1 = (bf16[32,1536]{1,0:T(8,128)(2,1)S(1)}, bf16[32,1536]{1,0:T(8,128)(2,1)}, u32[]{:S(2)}, u32[]{:S(2)}) collective-permute-start(bf16[32,1536]{1,0:T(8,128)(2,1)S(1)} %get-tuple-element.3), channel_id=1, source_target_pairs={{1,0},{2,1},{3,2},{4,3},{5,4},{6,5},{7,6},{9,8},{10,9},{11,10},{12... | collective-permute-start | bytes 294920 | tf_op jit(solution)/shard_map/ppermute | solution.py:17
  82.3 2.9 copy-start.1
  85.1 1.9 copy-start.8
  85.2 1.9 copy-start.9
  116.6 26.6 %copy-start.7 = (bf16[1,512,512]{2,1,0:T(8,128)(2,1)S(1)}, bf16[1,512,512]{2,1,0:T(8,128)(2,1)}, u32[]{:S(2)}) copy-start(bf16[1,512,512]{2,1,0:T(8,128)(2,1)} %param.19) | copy-start | bytes 1572868
  140.3 3.0 copy-start.11
  143.3 2.8 copy-start.13
  146.2 187.3 %all-gather.13.cloned.1.call-start = ((), (), s32[]{:S(2)}) async-start(), calls=%async_computation.5 | async-start | bytes 9830400 | tf_op jit(solution)/shard_map/all_gather | solution.py:110
  188.5 3.8 %copy-start.5 = (bf16[512,1536]{1,0:T(8,128)(2,1)S(1)}, bf16[512,1536]{1,0:T(8,128)(2,1)}, u32[]{:S(2)}) copy-start(bf16[512,1536]{1,0:T(8,128)(2,1)} %all-gather.11.cloned.1.call-done) | copy-start | bytes 4718596
  192.2 3.1 copy-start.6
  192.3 3.1 copy-start.12
  195.3 5.6 %copy-start.2 = (bf16[1536,3,384]{2,0,1:T(8,128)(2,1)S(1)}, bf16[1536,3,384]{2,0,1:T(8,128)(2,1)}, u32[]{:S(2)}) copy-start(bf16[1536,3,384]{2,0,1:T(8,128)(2,1)} %all-gather.7.cloned.1.call-done) | copy-start | bytes 10616836
  196.6 6.4 %collective-permute-start.2 = (bf16[32,384]{1,0:T(8,128)(2,1)S(1)}, bf16[32,384]{1,0:T(8,128)(2,1)S(1)}, u32[]{:S(2)}, u32[]{:S(2)}) collective-permute-start(bf16[32,384]{1,0:T(8,128)(2,1)S(1)} %get-tuple-element.4), channel_id=1, source_target_pairs={{1,0},{2,1},{3,2},{4,3},{5,4},{6,5},{7,6},{9,8},{10,9},{11,10},{12... | collective-permute-start | bytes 73736 | tf_op jit(solution)/shard_map/ppermute | solution.py:17
  197.9 4.1 %collective-permute-start.3 = (bf16[32,384]{1,0:T(8,128)(2,1)S(1)}, bf16[32,384]{1,0:T(8,128)(2,1)S(1)}, u32[]{:S(2)}, u32[]{:S(2)}) collective-permute-start(bf16[32,384]{1,0:T(8,128)(2,1)S(1)} %get-tuple-element.5), channel_id=1, source_target_pairs={{0,1},{1,2},{2,3},{3,4},{4,5},{5,6},{6,7},{8,9},{9,10},{10,11},{11... | collective-permute-start | bytes 73736 | tf_op jit(solution)/shard_map/ppermute | solution.py:16
Sparse Core Ops, SparseCore 0:
  9.6 72.6 all-gather.6
  83.9 29.0 all-gather.8
  115.4 24.7 all-gather.10
  146.3 38.4 reduce-scatter.1
  192.4 141.0 all-gather.12
